TPU v7x, 256 devices: a whole 4x4x8 slice. The times are simulated.
256 devices in a mesh: pb: 8 (over x, core), ka: 32 (over y, z).
Axes of the slice: x: 4, y: 4, z: 8, core: 2. Of those that a mesh axis runs over, the one named last changes fastest.
Arguments:
- queries: bfloat16 [64, 32768], P(None, ('pb', 'ka')), may hold values from -6 to 6
- keys: bfloat16 [64, 32768], P(None, ('ka', 'pb')), may hold values from -6 to 6
- values: bfloat16 [64, 32768], P(None, ('ka', 'pb')), may hold values from -7.5 to 7.5
- out_grads: bfloat16 [64, 32768], P(None, ('pb', 'ka')), may hold values from -7.5 to 7.5
- row_scales: bfloat16 [3, 32768], P(None, ('pb', 'ka')), as said below
- column_scales: bfloat16 [3, 32768], P(None, ('ka', 'pb')), as said below
Outputs:
- grad_queries: float32 [64, 32768], P(None, ('pb', 'ka'))
- grad_keys: float32 [64, 32768], P(None, ('ka', 'pb'))
- grad_values: float32 [64, 32768], P(None, ('ka', 'pb'))
Inputs may be any that keep to these rules, and one draw needn't show every extreme that they name: `row_scales`: positive. `column_scales`: positive.
All inputs are finite; a program needn't handle non-finite values.
Results may differ from a plain program's by a relative error of at most 0.0021.
Values may be sent and summed in bfloat16 or wider, within the bound.
A program may use at most 128 MiB of HBM per device.

v0:
```python
import jax
import jax.numpy as jnp
from jax import lax
from jax.sharding import PartitionSpec as P

HIGH = lax.Precision.HIGHEST


def body(queries, keys, values, out_grads, row_scales, column_scales):
    query_block, grad_block, row_block = (
        lax.all_gather(queries, "ka", axis=1, tiled=True),
        lax.all_gather(out_grads, "ka", axis=1, tiled=True),
        lax.all_gather(row_scales, "ka", axis=1, tiled=True),
    )
    key_block, value_block, column_block = (
        lax.all_gather(keys, "pb", axis=1, tiled=True),
        lax.all_gather(values, "pb", axis=1, tiled=True),
        lax.all_gather(column_scales, "pb", axis=1, tiled=True),
    )
    iters = row_block.shape[0]
    scale = query_block.shape[0] ** (-0.5)
    a = row_block.astype(jnp.float32)
    b = column_block.astype(jnp.float32)
    contract_first = (((0,), (0,)), ((), ()))
    scores = lax.dot_general(
        query_block, key_block, contract_first, preferred_element_type=jnp.float32
    )
    stored = jnp.exp(scores * scale)

    def tile():
        return stored

    dprobs = lax.dot_general(
        grad_block, value_block, contract_first, preferred_element_type=jnp.float32
    )
    a_last = a[iters - 1]
    b_last = b[iters - 1]
    weighted = tile() * (a_last[:, None] * b_last[None, :]) * dprobs
    probs = (tile() * (a_last[:, None] * b_last[None, :])).astype(jnp.bfloat16)
    value_part = lax.dot_general(
        grad_block, probs, (((1,), (0,)), ((), ())), preferred_element_type=jnp.float32
    )
    column_total = lax.psum(jnp.sum(weighted, 0), "pb")
    row_part = jnp.sum(weighted, 1)
    dg = [None] * (iters + 1)
    df = [None] * (iters + 1)
    dg[iters] = -column_total
    local = a_last * jnp.dot(tile(), b_last * dg[iters], precision=HIGH)
    row_total = lax.psum(row_part, "ka")
    df[iters] = -row_total - lax.psum(local, "ka")
    for t in range(iters - 1, 0, -1):
        column_sum = lax.psum(jnp.dot(a[t] * df[t + 1], tile(), precision=HIGH), "pb")
        dg[t] = -b[t - 1] * column_sum
        row_sum = lax.psum(jnp.dot(tile(), b[t - 1] * dg[t], precision=HIGH), "ka")
        df[t] = -a[t - 1] * row_sum
    ones = jnp.ones_like(b_last)
    bracket = a_last[:, None] * (b_last[None, :] * (dprobs + dg[iters][None, :]))
    for t in range(1, iters + 1):
        before = ones if t == 1 else b[t - 2]
        bracket = bracket + a[t - 1][:, None] * (before[None, :] * df[t][:, None])
    for t in range(1, iters):
        bracket = bracket + a[t - 1][:, None] * (b[t - 1][None, :] * dg[t][None, :])
    dscores = (tile() * bracket).astype(jnp.bfloat16)
    query_part = (
        lax.dot_general(
            key_block, dscores, (((1,), (1,)), ((), ())), preferred_element_type=jnp.float32
        )
        * scale
    )
    key_part = (
        lax.dot_general(
            query_block, dscores, (((1,), (0,)), ((), ())), preferred_element_type=jnp.float32
        )
        * scale
    )
    grad_keys, grad_values = (
        lax.psum_scatter(key_part, "pb", scatter_dimension=1, tiled=True),
        lax.psum_scatter(value_part, "pb", scatter_dimension=1, tiled=True),
    )
    grad_queries = lax.psum_scatter(query_part, "ka", scatter_dimension=1, tiled=True)
    return (grad_queries, grad_keys, grad_values)


def solution(mesh):
    in_specs = (
        P(None, ("pb", "ka")),
        P(None, ("ka", "pb")),
        P(None, ("ka", "pb")),
        P(None, ("pb", "ka")),
        P(None, ("pb", "ka")),
        P(None, ("ka", "pb")),
    )
    out_specs = (P(None, ("pb", "ka")), P(None, ("ka", "pb")), P(None, ("ka", "pb")))
    return jax.shard_map(body, mesh=mesh, in_specs=in_specs, out_specs=out_specs, check_vma=False)
```

profile of v0, /device:TPU:1, one launch (start us, length us, event | category | flops | bytes accessed | tf_op | source)
XLA Modules:
  0.0 997.7 jit_solution(15274470241596165231)
XLA Ops:
  7.2 12.1 %all_gather.21 = bf16[3,1024]{1,0:T(4,128)(2,1)S(1)} all-gather(bf16[3,128]{1,0:T(4,128)(2,1)} %param.11), channel_id=1, replica_groups=mesh['pb'=8,'ka'=32] {'pb'}, dimensions={1}, use_global_device_ids=true | all-gather | bytes 6912 | tf_op jit(solution)/shard_map/all_gather | solution.py:18
  19.3 36.2 %all_gather.20 = bf16[3,4096]{1,0:T(4,128)(2,1)S(1)} all-gather(bf16[3,128]{1,0:T(4,128)(2,1)} %param.10), channel_id=1, replica_groups=mesh['pb'=8,'ka'=32] {'ka'}, dimensions={1}, use_global_device_ids=true | all-gather | bytes 25344 | tf_op jit(solution)/shard_map/all_gather | solution.py:13
  55.6 21.5 %all_gather.19 = bf16[64,1024]{1,0:T(8,128)(2,1)S(1)} all-gather(bf16[64,128]{1,0:T(8,128)(2,1)} %param.7), channel_id=1, replica_groups=mesh['pb'=8,'ka'=32] {'pb'}, dimensions={1}, use_global_device_ids=true | all-gather | bytes 147456 | tf_op jit(solution)/shard_map/all_gather | solution.py:16
  77.1 36.8 %all_gather.18 = bf16[64,4096]{1,0:T(8,128)(2,1)S(1)} all-gather(bf16[64,128]{1,0:T(8,128)(2,1)} %param.6), channel_id=1, replica_groups=mesh['pb'=8,'ka'=32] {'ka'}, dimensions={1}, use_global_device_ids=true | all-gather | bytes 540672 | tf_op jit(solution)/shard_map/all_gather | solution.py:11
  113.9 36.5 %all_gather.22 = bf16[64,4096]{1,0:T(8,128)(2,1)S(1)} all-gather(bf16[64,128]{1,0:T(8,128)(2,1)} %param.9), channel_id=1, replica_groups=mesh['pb'=8,'ka'=32] {'ka'}, dimensions={1}, use_global_device_ids=true | all-gather | bytes 540672 | tf_op jit(solution)/shard_map/all_gather | solution.py:12
  152.9 5.7 copy-done
  161.4 35.3 %all_gather.23 = bf16[64,1024]{1,0:T(8,128)(2,1)S(1)} all-gather(bf16[64,128]{1,0:T(8,128)(2,1)S(1)} %copy-done.2), channel_id=1, replica_groups=mesh['pb'=8,'ka'=32] {'pb'}, dimensions={1}, use_global_device_ids=true | all-gather | bytes 147456 | tf_op jit(solution)/shard_map/all_gather | solution.py:17
  196.7 10.9 %fusion.7 = (f32[4096]{0:T(1024)S(1)}, f32[1024]{0:T(1024)S(1)}, f32[4096,1024]{1,0:T(8,128)}) fusion(f32[4096,1024]{1,0:T(8,128)} %copy-done, f32[1024]{0:T(1024)S(1)} %bitcast.58, f32[4096]{0:T(1024)S(1)} %bitcast.46, bf16[64,4096]{1,0:T(8,128)(2,1)S(1)} %all_gather.22, bf16[64,1024]{1,0:T(8,128)(2,1)S(1)} %all_gather.23), kind=kOutput, calls=%fused_computation.10 | convolution fusion | flops 557837312 | bytes 34250752 | tf_op jit(solution)/shard_map/dot_general | solution.py:33
  207.6 12.4 %psum.49 = f32[1024]{0:T(1024)S(1)} all-reduce(f32[1024]{0:T(1024)S(1)} %get-tuple-element.4), channel_id=1, replica_groups=mesh['pb'=8,'ka'=32] {'pb'}, use_global_device_ids=true, to_apply=%region_1.0 | all-reduce | flops 1024 | bytes 8192 | tf_op jit(solution)/shard_map/psum | solution.py:43
  220.0 17.5 %fusion.20 = f32[1,4096]{1,0:T(1,128)S(1)} fusion(f32[4096,1024]{1,0:T(8,128)} %copy-done, f32[1024,1]{0,1:T(1,128)S(1)} %bitcast.69), kind=kOutput, calls=%fused_computation.30 | convolution fusion | flops 50331648 | bytes 16797696 | tf_op jit(solution)/shard_map/dot_general | solution.py:48
  237.5 112.8 %all-reduce = (f32[4096]{0:T(1024)S(1)}, f32[4096]{0:T(1024)S(1)}) all-reduce(f32[4096]{0:T(1024)S(1)} %mul.201, f32[4096]{0:T(1024)S(1)} %get-tuple-element.3), channel_id=1, replica_groups=mesh['pb'=8,'ka'=32] {'ka'}, use_global_device_ids=true, to_apply=%region_4.0 | all-reduce | flops 8192 | bytes 65536 | tf_op jit(solution)/shard_map/psum | solution.py:50
  350.3 11.5 %fusion.21 = f32[1,1024]{1,0:T(1,128)S(1)} fusion(f32[4096,1]{0,1:T(1,128)S(1)} %bitcast.61, f32[4096,1024]{1,0:T(8,128)} %copy-done), kind=kOutput, calls=%fused_computation.31 | convolution fusion | flops 50331648 | bytes 16797696 | tf_op jit(solution)/shard_map/dot_general | solution.py:52
  361.7 40.5 %psum.52 = f32[1024]{0:T(1024)S(1)} all-reduce(f32[1024]{0:T(1024)S(1)} %bitcast.74), channel_id=1, replica_groups=mesh['pb'=8,'ka'=32] {'pb'}, use_global_device_ids=true, to_apply=%region_5.0 | all-reduce | flops 1024 | bytes 8192 | tf_op jit(solution)/shard_map/psum | solution.py:52
  402.2 17.5 %fusion.22 = f32[1,4096]{1,0:T(1,128)S(1)} fusion(f32[4096,1024]{1,0:T(8,128)} %copy-done, f32[1024,1]{0,1:T(1,128)S(1)} %bitcast.70), kind=kOutput, calls=%fused_computation.32 | convolution fusion | flops 50331648 | bytes 16797696 | tf_op jit(solution)/shard_map/dot_general | solution.py:54
  419.7 109.9 %psum.53 = f32[4096]{0:T(1024)S(1)} all-reduce(f32[4096]{0:T(1024)S(1)} %bitcast.55), channel_id=1, replica_groups=mesh['pb'=8,'ka'=32] {'ka'}, use_global_device_ids=true, to_apply=%region_6.0 | all-reduce | flops 4096 | bytes 32768 | tf_op jit(solution)/shard_map/psum | solution.py:54
  529.6 11.5 %fusion.23 = f32[1,1024]{1,0:T(1,128)S(1)} fusion(f32[4096,1]{0,1:T(1,128)S(1)} %bitcast.62, f32[4096,1024]{1,0:T(8,128)} %copy-done), kind=kOutput, calls=%fused_computation.33 | convolution fusion | flops 50331648 | bytes 16797696 | tf_op jit(solution)/shard_map/dot_general | solution.py:52
  541.1 40.4 %psum.54 = f32[1024]{0:T(1024)S(1)} all-reduce(f32[1024]{0:T(1024)S(1)} %bitcast.75), channel_id=1, replica_groups=mesh['pb'=8,'ka'=32] {'pb'}, use_global_device_ids=true, to_apply=%region_7.0 | all-reduce | flops 1024 | bytes 8192 | tf_op jit(solution)/shard_map/psum | solution.py:52
  581.5 17.5 %fusion.24 = f32[1,4096]{1,0:T(1,128)S(1)} fusion(f32[4096,1024]{1,0:T(8,128)} %copy-done, f32[1024,1]{0,1:T(1,128)S(1)} %bitcast.71), kind=kOutput, calls=%fused_computation.34 | convolution fusion | flops 50331648 | bytes 16797696 | tf_op jit(solution)/shard_map/dot_general | solution.py:54
  599.0 109.9 %psum.55 = f32[4096]{0:T(1024)S(1)} all-reduce(f32[4096]{0:T(1024)S(1)} %bitcast.56), channel_id=1, replica_groups=mesh['pb'=8,'ka'=32] {'ka'}, use_global_device_ids=true, to_apply=%region_8.0 | all-reduce | flops 4096 | bytes 32768 | tf_op jit(solution)/shard_map/psum | solution.py:54
  708.9 12.7 %multiply_convert_fusion = bf16[4096,1024]{1,0:T(8,128)(2,1)S(1)} fusion(f32[4096,1024]{1,0:T(8,128)} %copy-done, f32[4096,1024]{1,0:T(8,128)} %get-tuple-element.25, f32[1024]{0:T(1024)S(1)} %bitcast.68, f32[1024]{0:T(1024)S(1)} %bitcast.67, f32[4096]{0:T(1024)S(1)} %bitcast.51, f32[4096]{0:T(1024)S(1)} %get-tuple-element.8, f32[1024]{0:T(1024)S(1)} %bitcast.66, ...), kind=kLoop, calls=%fused_computation | loop fusion | flops 67108864 | bytes 42065920 | tf_op jit(solution)/shard_map/convert_element_type | solution.py:63
  721.6 3.2 copy-done.1
  727.2 7.1 fusion.6
  734.4 42.2 %reduce-scatter.6.cloned.1.call-done = f32[64,128]{1,0:T(8,128)} async-done(((f32[64,1024]{1,0:T(8,128)}), f32[64,128]{1,0:T(8,128)}) %reduce-scatter.6.cloned.1.call-update) | async-done | bytes 32784 | tf_op jit(solution)/shard_map/reduce_scatter | solution.py:77
  776.6 214.3 %reduce-scatter.4.cloned.1.call-done = f32[64,128]{1,0:T(8,128)} async-done(((f32[64,4096]{1,0:T(8,128)}), f32[64,128]{1,0:T(8,128)}) %reduce-scatter.4.cloned.1.call-update) | async-done | bytes 32784 | tf_op jit(solution)/shard_map/reduce_scatter | solution.py:80
  (25 shorter events, 7.8 us)
Async XLA Ops:
  7.2 727.2 %reduce-scatter.8.cloned.1.call-start = ((), (), s32[]{:S(2)}) async-start(), calls=%async_computation.5 | async-start | bytes 294912 | tf_op jit(solution)/shard_map/reduce_scatter | solution.py:78
  150.4 11.0 %copy-start.2 = (bf16[64,128]{1,0:T(8,128)(2,1)S(1)}, bf16[64,128]{1,0:T(8,128)(2,1)}, u32[]{:S(2)}) copy-start(bf16[64,128]{1,0:T(8,128)(2,1)} %param.8) | copy-start | bytes 49156
  152.9 5.7 copy-start
  161.3 615.3 %reduce-scatter.6.cloned.1.call-start = ((), (), s32[]{:S(2)}) async-start(), calls=%async_computation.4 | async-start | bytes 294912 | tf_op jit(solution)/shard_map/reduce_scatter | solution.py:77
  721.6 3.2 copy-start.1
  727.2 263.7 %reduce-scatter.4.cloned.1.call-start = ((), (), s32[]{:S(2)}) async-start(), calls=%async_computation.3 | async-start | bytes 1081344 | tf_op jit(solution)/shard_map/reduce_scatter | solution.py:80
Sparse Core Ops, SparseCore 0:
  161.4 51.3 reduce-scatter.7
  727.3 49.2 reduce-scatter.5
  781.0 209.8 reduce-scatter.3
where the time goes:
time: 1010 us; the launch traced here: 998 us
  blocking collectives  604 us (60%)
  waiting for transfers between devices  257 us (25%)
  matrix products  101 us (10%)
  between operations  14.1 us (1%)
  other arithmetic  12.8 us (1%)
    psum x2, blocking collectives, body(): row_sum = lax.psum(jnp.dot(tile(), b[t - 1] * dg[t], precision=HIGH), 'ka')  220 us
    reduce_scatter x1, waiting for transfers between devices, body(): lax.psum_scatter(query_part, 'ka', scatter_dimension=1, tiled=True)  214 us
    psum x1, blocking collectives, body(): df[iters] = -row_total - lax.psum(local, 'ka')  113 us
    psum x2, blocking collectives, body(): lax.psum(jnp.dot(a[t] * df[t + 1], tile(), precision=HIGH), 'pb')  80.9 us
    reduce_scatter x1, waiting for transfers between devices, body(): lax.psum_scatter(key_part, 'pb', scatter_dimension=1, tiled=True)  42.2 us
    all_gather x1, blocking collectives, body(): lax.all_gather(queries, 'ka', axis=1, tiled=True)  36.8 us
    all_gather x1, blocking collectives, body(): lax.all_gather(out_grads, 'ka', axis=1, tiled=True)  36.5 us
    all_gather x1, blocking collectives, body(): lax.all_gather(row_scales, 'ka', axis=1, tiled=True)  36.2 us
  transfers between devices with their start and end apart: 3, of which 2 were waited for; matrix products, arithmetic and copies ran while one was open for 11% of the time, Pallas kernels for 0%

commit v1 on v0

v1 whole, which is shorter than its diff:
```python
import functools
import math

import jax
import jax.numpy as jnp
from jax import lax
from jax.experimental import pallas as pl
from jax.experimental.pallas import tpu as pltpu
from jax.sharding import PartitionSpec as P

F32, BF16 = jnp.float32, jnp.bfloat16
MESH = pl.DeviceIdType.MESH
GROUP = 16
BLOCK = 128
HEAD = 64
LONG = GROUP * BLOCK
MSG = 2 * HEAD + 16
SCALE = HEAD ** -0.5
EXP2_SCALE = SCALE * math.log2(math.e)
JT, IT = 256, 512
LOW = 3 * HEAD


def split3(x):
    hi = x.astype(BF16).astype(F32)
    rest = x - hi
    mid = rest.astype(BF16).astype(F32)
    return hi, mid, rest - mid


def kernel(
    q_ref, k_ref, v_ref, g_ref, rs_ref, cs_ref,
    gq_ref, gk_ref, gv_ref,
    qall, kall, kern, kT, lj, fi, fif, ljf, qcat, gcat, kcat,
    a_p, b_p, vec, ub, b3b, w8, r8, cacc, ar,
    gqp, gkp, gvp, gqr, gkr, gvr,
    send_sem, recv_sem,
):
    pb, ka = lax.axis_index("pb"), lax.axis_index("ka")
    x, core, y, z = pb // 2, pb % 2, ka // 8, ka % 8
    me_a = z * 2 + core
    me_b = x * 4 + y

    def dev_a(p):
        return (x * 2 + p % 2, y * 8 + p // 2)

    def dev_b(p):
        return ((p // 4) * 2 + core, (p % 4) * 8 + z)

    barrier = pltpu.get_barrier_semaphore()

    def greet(d, _):
        pl.semaphore_signal(barrier, inc=1, device_id=dev_a((me_a + d) % GROUP), device_id_type=MESH)
        pl.semaphore_signal(barrier, inc=1, device_id=dev_b((me_b + d) % GROUP), device_id_type=MESH)
        return 0

    lax.fori_loop(1, GROUP, greet, 0)

    pad = jnp.zeros((13, BLOCK), F32)
    qall[me_a, 0:HEAD, :] = q_ref[...]
    qall[me_a, HEAD:2 * HEAD, :] = g_ref[...]
    qall[me_a, 2 * HEAD:MSG, :] = jnp.concatenate([rs_ref[...].astype(F32), pad], 0).astype(BF16)
    kall[me_b, 0:HEAD, :] = k_ref[...]
    kall[me_b, HEAD:2 * HEAD, :] = v_ref[...]
    kall[me_b, 2 * HEAD:MSG, :] = jnp.concatenate([cs_ref[...].astype(F32), pad], 0).astype(BF16)
    pl.semaphore_wait(barrier, 2 * (GROUP - 1))

    def copy(src, dst, n, device):
        return pltpu.make_async_remote_copy(
            src_ref=src, dst_ref=dst, send_sem=send_sem.at[n], recv_sem=recv_sem.at[n],
            device_id=device, device_id_type=MESH,
        )

    def broadcast(buf, me, dev, n):
        def go(d, _):
            copy(buf.at[me], buf.at[me], n, dev((me + d) % GROUP)).start()
            return 0
        lax.fori_loop(1, GROUP, go, 0)

    def scatter(buf, got, me, dev, n):
        def go(d, _):
            p = (me + d) % GROUP
            copy(buf.at[p], got.at[me], n, dev(p)).start()
            return 0
        lax.fori_loop(1, GROUP, go, 0)

    def wait_recv(buf, n):
        part = buf.at[pl.ds(0, GROUP - 1)]
        pltpu.make_async_copy(part, part, recv_sem.at[n]).wait()

    def wait_send(buf, n):
        part = buf.at[pl.ds(0, GROUP - 1)]
        pltpu.make_async_copy(part, part, send_sem.at[n]).wait()

    broadcast(kall, me_b, dev_b, 0)
    broadcast(qall, me_a, dev_a, 1)
    fif[...] = jnp.zeros_like(fif)
    ljf[...] = jnp.zeros_like(ljf)
    r8[...] = jnp.zeros_like(r8)

    wait_recv(kall, 0)

    def lanes(b):
        return pl.ds(pl.multiple_of(b * BLOCK, BLOCK), BLOCK)

    def prep_keys(b, _):
        at = lanes(b)
        kb = kall[b, 0:HEAD, :]
        kcat[:, at] = kb
        scales = kall[b, 2 * HEAD:MSG, :].astype(F32)
        for t in range(3):
            b_p[t, pl.ds(b, 1), :] = scales[t:t + 1]
        bv = kall[b, HEAD:2 * HEAD, :].astype(F32) * scales[2:3]
        hi = bv.astype(BF16).astype(F32)
        lo = bv - hi
        zero = jnp.zeros((HEAD, BLOCK), F32)
        lj[at, 0:128] = jnp.concatenate([hi, hi], 0).T.astype(BF16)
        lj[at, 128:256] = jnp.concatenate([lo, zero], 0).T.astype(BF16)
        kT[at, :] = jnp.concatenate([kb.astype(F32), zero], 0).T[:, 0:HEAD].astype(BF16)
        b3b[at, :] = jnp.broadcast_to(scales[2:3], (BLOCK, BLOCK)).T
        return 0

    lax.fori_loop(0, GROUP, prep_keys, 0)
    wait_recv(qall, 1)

    def prep_queries(b, _):
        at = lanes(b)
        qcat[:, at] = qall[b, 0:HEAD, :]
        gb = qall[b, HEAD:2 * HEAD, :]
        gcat[:, at] = gb
        scales = qall[b, 2 * HEAD:MSG, :].astype(F32)
        for t in range(3):
            a_p[t, pl.ds(b, 1), :] = scales[t:t + 1]
        ag = gb.astype(F32) * scales[2:3]
        hi = ag.astype(BF16)
        lo = (ag - hi.astype(F32)).astype(BF16)
        fi[0:64, at] = hi
        fi[64:128, at] = lo
        fi[128:192, at] = hi
        fi[192:256, at] = jnp.zeros((HEAD, BLOCK), BF16)
        return 0

    lax.fori_loop(0, GROUP, prep_queries, 0)

    def tiles(body):
        def go(n, _):
            jt, it = n // (LONG // IT), n % (LONG // IT)
            body(jt, it, pl.ds(pl.multiple_of(jt * JT, JT), JT), pl.ds(pl.multiple_of(it * IT, IT), IT))
            return 0
        return go

    def first(jt, it, js, ls):
        s = jnp.dot(kT[js, :], qcat[:, ls], preferred_element_type=F32)
        e = jnp.exp2(s * EXP2_SCALE)
        kern[js, ls] = e
        w = e * jnp.dot(lj[js, :], fi[:, ls], preferred_element_type=F32)
        r8[:, ls] += jnp.sum(w.reshape(JT // 8, 8, IT), 0)
        part = w[:, 0:128]
        for n in range(1, IT // 128):
            part = part + w[:, n * 128:(n + 1) * 128]

        @pl.when(it == 0)
        def _():
            cacc[js, :] = part

        @pl.when(it > 0)
        def _():
            cacc[js, :] += part

    lax.fori_loop(0, (LONG // JT) * (LONG // IT), tiles(first), 0)

    def column_block(b, acc, r):
        ar[r, me_b, pl.ds(b, 1), :] = jnp.sum(acc.T, 0, keepdims=True)

    def column_first(b, _):
        column_block(b, cacc[lanes(b), :], 0)
        return 0

    lax.fori_loop(0, GROUP, column_first, 0)

    def total(r):
        return jnp.sum(ar[r], 0)

    def spread_keys():
        def go(b, _):
            ub[lanes(b), :] = jnp.broadcast_to(vec[pl.ds(b, 1), :], (BLOCK, BLOCK)).T
            return 0
        lax.fori_loop(0, GROUP, go, 0)

    def spread_queries():
        for b in range(GROUP):
            w8[:, b * 128:(b + 1) * 128] = jnp.broadcast_to(vec[b:b + 1, :], (8, BLOCK))

    def column_apply(r):
        def go(b, _):
            at = lanes(b)
            acc = kern[at, 0:128] * w8[0:1, 0:128]
            for n in range(1, GROUP):
                acc = acc + kern[at, n * 128:(n + 1) * 128] * w8[0:1, n * 128:(n + 1) * 128]
            column_block(b, acc, r)
            return 0
        lax.fori_loop(0, GROUP, go, 0)

    WIDE = 8

    def row_apply(store):
        for half in range(GROUP // WIDE):
            def go(c, accs):
                js = pl.ds(pl.multiple_of(c * 64, 64), 64)
                u = ub[js, :]
                new = []
                for n in range(WIDE):
                    o = (half * WIDE + n) * 128
                    prod = kern[js, o:o + 128] * u
                    new.append(accs[n] + jnp.sum(prod.reshape(8, 8, 128), 0))
                return tuple(new)
            accs = lax.fori_loop(0, LONG // 64, go, tuple(jnp.zeros((8, BLOCK), F32) for _ in range(WIDE)))
            for n in range(WIDE):
                store(half * WIDE + n, accs[n])

    def grad_value_tiles(j0, j1):
        def body(jt, it, js, ls):
            b3 = b3b[js, :]
            a3 = fif[63:64, ls]
            probs = (kern[js, ls] * (a3 * jnp.concatenate([b3] * (IT // 128), 1))).astype(BF16)
            part = lax.dot_general(gcat[:, ls], probs, (((1,), (1,)), ((), ())), preferred_element_type=F32)
            for n in range(JT // 128):
                at = jt * (JT // 128) + n

                @pl.when(it == 0)
                def _():
                    gvp[at] = part[:, n * 128:(n + 1) * 128]

                @pl.when(it > 0)
                def _():
                    gvp[at] += part[:, n * 128:(n + 1) * 128]
        lax.fori_loop(j0 * (LONG // IT), j1 * (LONG // IT), tiles(body), 0)

    def put_rows(dst, rows, value):
        for n, piece in zip(rows, value):
            vec[...] = piece
            for b in range(GROUP):
                dst[n:n + 1, b * 128:(b + 1) * 128] = vec[b:b + 1, :]

    broadcast(ar.at[0], me_b, dev_b, 2)
    put_rows(fif, [63], [a_p[2]])
    for n, t in ((0, 2), (3, 1), (6, 0)):
        put_rows(fif, [n, n + 1, n + 2], [a_p[t]] * 3)
    for n, t in ((9, 1), (12, 0)):
        put_rows(ljf, [n, n + 1, n + 2], [b_p[t]] * 3)
    ljf[15:18, :] = jnp.ones((3, LONG), F32)
    grad_value_tiles(0, 2)

    for t in (2, 1, 0):
        r = 2 * (2 - t)
        wait_recv(ar.at[r], 2 + r)
        dg = -total(r)
        if t < 2:
            dg = b_p[t] * dg
        bdg = b_p[t] * dg
        vec[...] = bdg
        spread_keys()
        if t == 2:
            def store(n, acc):
                a = a_p[2, n:n + 1, :]
                ar[1, me_a, n:n + 1, :] = a * jnp.sum(acc, 0, keepdims=True) + jnp.sum(
                    r8[:, n * 128:(n + 1) * 128], 0, keepdims=True)
        else:
            def store(n, acc, r=r):
                ar[r + 1, me_a, n:n + 1, :] = jnp.sum(acc, 0, keepdims=True)
        row_apply(store)
        broadcast(ar.at[r + 1], me_a, dev_a, 3 + r)
        put_rows(ljf, [3 * (2 - t) + n for n in range(3)], split3(bdg))
        if t == 2:
            grad_value_tiles(2, 5)
        elif t == 1:
            scatter(gvp, gvr, me_b, dev_b, 8)
        else:
            def late_keys(b, _):
                at = lanes(b)
                zero = jnp.zeros((HEAD, BLOCK), F32)
                low = jnp.concatenate([ljf[:, at], zero], 0).T[:, 0:HEAD]
                lj[at, LOW:LOW + HEAD] = low.astype(BF16)
                return 0
            lax.fori_loop(0, GROUP, late_keys, 0)
        wait_recv(ar.at[r + 1], 3 + r)
        df = -total(r + 1)
        if t < 2:
            df = a_p[t] * df
        adf = a_p[t] * df
        if t > 0:
            vec[...] = adf
            spread_queries()
            column_apply(r + 2)
            broadcast(ar.at[r + 2], me_b, dev_b, 4 + r)
            if t == 2:
                grad_value_tiles(5, 8)
        put_rows(fif, [9 + 3 * (2 - t) + n for n in range(3)], split3(adf))

    fi[LOW:LOW + HEAD, :] = fif[...].astype(BF16)
    gqp[...] = jnp.zeros_like(gqp)

    def last(jt, it, js, ls):
        bracket = jnp.dot(lj[js, :], fi[:, ls], preferred_element_type=F32)
        ds = (kern[js, ls] * bracket).astype(BF16)
        part = jnp.dot(kcat[:, js], ds, preferred_element_type=F32)
        for n in range(IT // 128):
            gqp[it * (IT // 128) + n] += part[:, n * 128:(n + 1) * 128]
        part = lax.dot_general(qcat[:, ls], ds, (((1,), (1,)), ((), ())), preferred_element_type=F32)
        for n in range(JT // 128):
            at = jt * (JT // 128) + n

            @pl.when(it == 0)
            def _():
                gkp[at] = part[:, n * 128:(n + 1) * 128]

            @pl.when(it > 0)
            def _():
                gkp[at] += part[:, n * 128:(n + 1) * 128]

    lax.fori_loop(0, (LONG // JT) * (LONG // IT), tiles(last), 0)

    scatter(gqp, gqr, me_a, dev_a, 9)
    scatter(gkp, gkr, me_b, dev_b, 10)
    gvr[me_b] = gvp[me_b]
    gqr[me_a] = gqp[me_a]
    gkr[me_b] = gkp[me_b]
    wait_recv(gvr, 8)
    gv_ref[...] = jnp.sum(gvr[...], 0)
    wait_recv(gqr, 9)
    gq_ref[...] = jnp.sum(gqr[...], 0) * SCALE
    wait_recv(gkr, 10)
    gk_ref[...] = jnp.sum(gkr[...], 0) * SCALE
    wait_send(kall, 0)
    wait_send(qall, 1)
    for r in range(6):
        wait_send(ar.at[r], 2 + r)
    wait_send(gvp, 8)
    wait_send(gqp, 9)
    wait_send(gkp, 10)


def body(queries, keys, values, out_grads, row_scales, column_scales):
    out = jax.ShapeDtypeStruct((HEAD, BLOCK), F32)
    vmem = pl.BlockSpec(memory_space=pltpu.VMEM)
    part = pltpu.VMEM((GROUP, HEAD, BLOCK), F32)
    return pl.pallas_call(
        kernel,
        out_shape=(out, out, out),
        in_specs=[vmem] * 6,
        out_specs=(vmem,) * 3,
        scratch_shapes=[
            pltpu.VMEM((GROUP, MSG, BLOCK), BF16),
            pltpu.VMEM((GROUP, MSG, BLOCK), BF16),
            pltpu.VMEM((LONG, LONG), F32),
            pltpu.VMEM((LONG, HEAD), BF16),
            pltpu.VMEM((LONG, 4 * HEAD), BF16),
            pltpu.VMEM((4 * HEAD, LONG), BF16),
            pltpu.VMEM((HEAD, LONG), F32),
            pltpu.VMEM((HEAD, LONG), F32),
            pltpu.VMEM((HEAD, LONG), BF16),
            pltpu.VMEM((HEAD, LONG), BF16),
            pltpu.VMEM((HEAD, LONG), BF16),
            pltpu.VMEM((3, GROUP, BLOCK), F32),
            pltpu.VMEM((3, GROUP, BLOCK), F32),
            pltpu.VMEM((GROUP, BLOCK), F32),
            pltpu.VMEM((LONG, BLOCK), F32),
            pltpu.VMEM((LONG, BLOCK), F32),
            pltpu.VMEM((8, LONG), F32),
            pltpu.VMEM((8, LONG), F32),
            pltpu.VMEM((LONG, BLOCK), F32),
            pltpu.VMEM((6, GROUP, GROUP, BLOCK), F32),
            part, part, part, part, part, part,
            pltpu.SemaphoreType.DMA((11,)),
            pltpu.SemaphoreType.DMA((11,)),
        ],
        compiler_params=pltpu.CompilerParams(
            collective_id=0, has_side_effects=True, vmem_limit_bytes=56 * 2**20),
    )(queries, keys, values, out_grads, row_scales, column_scales)


def solution(mesh):
    in_specs = (
        P(None, ("pb", "ka")),
        P(None, ("ka", "pb")),
        P(None, ("ka", "pb")),
        P(None, ("pb", "ka")),
        P(None, ("pb", "ka")),
        P(None, ("ka", "pb")),
    )
    out_specs = (P(None, ("pb", "ka")), P(None, ("ka", "pb")), P(None, ("ka", "pb")))
    return jax.shard_map(body, mesh=mesh, in_specs=in_specs, out_specs=out_specs, check_vma=False)
```

time: 1010 us -> 121 us (0.12); the launches traced: 998 us -> 121 us
  blocking collectives: 604 us -> 0 us
  waiting for transfers between devices: 257 us -> 0 us
  Pallas kernels: 0 us -> 118 us
  matrix products: 101 us -> 0 us
  between operations: 14.1 us -> 0.65 us
  other arithmetic: 12.8 us -> 0 us
    psum x6 -> x0, blocking collectives: 426 us -> none  [the longest x2 220 us: body(): row_sum = lax.psum(jnp.dot(tile(), b[t - 1] * dg[t], precision=HIGH), 'ka')]
    reduce_scatter x3 -> x0, waiting for transfers between devices: 257 us -> none  [the longest x1 214 us: body(): lax.psum_scatter(query_part, 'ka', scatter_dimension=1, tiled=True)]
    all_gather x6 -> x0, blocking collectives: 178 us -> none  [the longest x1 36.8 us: body(): lax.all_gather(queries, 'ka', axis=1, tiled=True)]
    pallas_call x0 -> x1, Pallas kernels: none -> 118 us  [body(): pl.pallas_call(kernel, out_shape=(out, out, out), in_specs=[vmem] * 6, ou...]
    dot_general x10 -> x0, matrix products: 101 us -> none  [the longest x2 35 us: body(): row_sum = lax.psum(jnp.dot(tile(), b[t - 1] * dg[t], precision=HIGH), 'ka')]
    convert_element_type x2 -> x0, other arithmetic: 12.7 us -> none  [the longest x1 12.7 us: body(): dscores = (tile() * bracket).astype(jnp.bfloat16)]
  transfers between devices with their start and end apart: 3 -> 0, of which waited for: 2 -> 0; matrix products, arithmetic and copies ran while one was open for 11% -> 0% of each run, Pallas kernels for 0% -> 0%
where the time goes in v1:
time: 121 us
  Pallas kernels  118 us (98%)
  local copies, waits for them, and re-layouts  2.77 us (2%)
    pallas_call x1, Pallas kernels, body(): pl.pallas_call(kernel, out_shape=(out, out, out), in_specs=[vmem] * 6, ou...  118 us
    unnamed x7, local copies, waits for them, and re-layouts  2.77 us

profile of v1, /device:TPU:1, one launch (start us, length us, event | category | flops | bytes accessed | tf_op | source)
XLA Modules:
  0.0 121.2 jit_solution(14795360212291981564)
XLA Ops:
  0.6 117.7 %shard_map.85 = (f32[64,128]{1,0:T(8,128)}, f32[64,128]{1,0:T(8,128)}, f32[64,128]{1,0:T(8,128)}) custom-call(bf16[64,128]{1,0:T(8,128)(2,1)} %q_ref.1, bf16[64,128]{1,0:T(8,128)(2,1)} %k_ref.1, bf16[64,128]{1,0:T(8,128)(2,1)} %v_ref.1, bf16[64,128]{1,0:T(8,128)(2,1)} %g_ref.1, bf16[3,128]{1,0:T(4,128)(2,1)} %rs_ref.1, bf16[3,128]{1,0:T(4,128)(2,1)} %cs_ref.1), custom_call_target="tpu_custom_call" | custom-call | tf_op jit(solution)/shard_map/pallas_call | solution.py:347
  118.4 0.0 copy-start.1
  118.4 1.4 %copy.12 = f32[64,128]{1,0:T(8,128)} copy(f32[64,128]{1,0:T(8,128)} %get-tuple-element.6) | data formatting | bytes 65536
  119.8 0.0 copy-done.1
  119.8 0.0 copy-start
  119.8 0.6 copy.13
  120.4 0.2 copy-done
  120.5 0.6 copy.14
Async XLA Ops:
  118.4 1.4 %copy-start.1 = (f32[64,128]{1,0:T(8,128)S(1)}, f32[64,128]{1,0:T(8,128)}, u32[]{:S(2)}) copy-start(f32[64,128]{1,0:T(8,128)} %get-tuple-element.7) | copy-start | bytes 98308
  119.8 0.8 copy-start

commit v2 on v0

v2 whole, which is shorter than its diff:
```python
import math

import jax
import jax.numpy as jnp
from jax import lax
from jax.experimental import pallas as pl
from jax.experimental.pallas import tpu as pltpu
from jax.sharding import PartitionSpec as P

F32, BF16 = jnp.float32, jnp.bfloat16
MESH = pl.DeviceIdType.MESH
GROUP = 16
HALF = 8
BLOCK = 128
HEAD = 64
LONG = GROUP * BLOCK
WIDE = HALF * BLOCK
MSG = HEAD + 16
SCALE = HEAD ** -0.5
EXP2_SCALE = SCALE * math.log2(math.e)
LOW = 3 * HEAD
FAR_Z = (4, 3, 5, 2, 6, 1, 7)
FAR_ZC = tuple((dz, dc) for dz in FAR_Z for dc in (0, 1)) + ((0, 1),)
FAR_XY = ((2, 2), (1, 2), (2, 1), (3, 2), (2, 3), (1, 1), (3, 3), (1, 3), (3, 1),
          (0, 2), (2, 0), (0, 1), (1, 0), (0, 3), (3, 0))
K_IN, V_IN, Q_IN, G_IN, Q_SIB, G_SIB, AR, GV, GQ_SIB, GQ, GK = 0, 1, 2, 3, 4, 5, 6, 12, 13, 14, 15
N_SEM = 16


def split3(x):
    hi = x.astype(BF16).astype(F32)
    rest = x - hi
    mid = rest.astype(BF16).astype(F32)
    return hi, mid, rest - mid


def kernel(
    q_ref, k_ref, v_ref, g_ref, rs_ref, cs_ref,
    out_ref,
    qs, gs, ks, vs, kern, kT, qT, gT, lj, fi, fif, ljf, qcat, kcat,
    a_p, b_p, vec, ub, b3b, w8, r8, cacc, ar,
    gvt, gkt, gqp, gkp, gvp, gqs, gqr, gkr, gvr,
    send_sem, recv_sem,
):
    pb, ka = lax.axis_index("pb"), lax.axis_index("ka")
    x, core, y, z = pb // 2, pb % 2, ka // 8, ka % 8
    me_a = core * HALF + z
    me_b = x * 4 + y
    sibling = (x * 2 + 1 - core, ka)

    def dev_z(dz, dc):
        return (x * 2 + (core + dc) % 2, y * 8 + (z + dz) % 8)

    def dev_xy(dx, dy):
        return (((x + dx) % 4) * 2 + core, ((y + dy) % 4) * 8 + z)

    barrier = pltpu.get_barrier_semaphore()
    for d in FAR_XY:
        pl.semaphore_signal(barrier, inc=1, device_id=dev_xy(*d), device_id_type=MESH)
    for d in FAR_ZC:
        pl.semaphore_signal(barrier, inc=1, device_id=dev_z(*d), device_id_type=MESH)

    pad = jnp.zeros((13, BLOCK), F32)
    ks[me_b] = k_ref[...]
    qs[me_a] = q_ref[...]
    vs[me_b, 0:HEAD, :] = v_ref[...]
    vs[me_b, HEAD:MSG, :] = jnp.concatenate([cs_ref[...].astype(F32), pad], 0).astype(BF16)
    gs[me_a, 0:HEAD, :] = g_ref[...]
    gs[me_a, HEAD:MSG, :] = jnp.concatenate([rs_ref[...].astype(F32), pad], 0).astype(BF16)
    pl.semaphore_wait(barrier, 2 * (GROUP - 1))

    def send(src, dst, n, device):
        pltpu.make_async_remote_copy(
            src_ref=src, dst_ref=dst, send_sem=send_sem.at[n], recv_sem=recv_sem.at[n],
            device_id=device, device_id_type=MESH,
        ).start()

    def to_xy(buf, n):
        for d in FAR_XY:
            send(buf.at[me_b], buf.at[me_b], n, dev_xy(*d))

    def to_zc(buf, n):
        for d in FAR_ZC:
            send(buf.at[me_a], buf.at[me_a], n, dev_z(*d))

    def to_z(buf, n):
        for dz in FAR_Z:
            send(buf.at[me_a], buf.at[me_a], n, dev_z(dz, 0))

    def own_half(buf):
        return buf.at[pl.ds(pl.multiple_of(core * HALF, HALF), HALF)]

    def wait(sem, n, part):
        pltpu.make_async_copy(part, part, sem.at[n]).wait()

    def wait_recv(buf, n, count):
        wait(recv_sem, n, buf.at[pl.ds(0, count)])

    def wait_send(buf, n, count):
        wait(send_sem, n, buf.at[pl.ds(0, count)])

    to_xy(ks, K_IN)
    to_z(qs, Q_IN)
    to_xy(vs, V_IN)
    to_z(gs, G_IN)

    fif[...] = jnp.zeros_like(fif)
    ljf[...] = jnp.zeros_like(ljf)
    r8[...] = jnp.zeros_like(r8)
    fi[LOW:LOW + HEAD, :] = jnp.zeros((HEAD, LONG), BF16)
    zero = jnp.zeros((HEAD, BLOCK), F32)

    def turned(block):
        return jnp.concatenate([block.astype(F32), zero], 0).T[:, 0:HEAD]

    def lanes(b):
        return pl.ds(pl.multiple_of(b * BLOCK, BLOCK), BLOCK)

    wait_recv(ks, K_IN, GROUP - 1)
    for b in range(GROUP):
        kcat[:, b * BLOCK:(b + 1) * BLOCK] = ks[b]
        kT[b * BLOCK:(b + 1) * BLOCK, :] = turned(ks[b]).astype(BF16)

    def prep_q(h):
        for n in range(HALF):
            b = h * HALF + n
            qcat[:, lanes(b)] = qs[b]

    def prep_g(h):
        for n in range(HALF):
            b = h * HALF + n
            gb = gs[b, 0:HEAD, :]
            scales = gs[b, HEAD:MSG, :].astype(F32)
            for t in range(3):
                a_p[t, pl.ds(b, 1), :] = scales[t:t + 1]
            ag = gb.astype(F32) * scales[2:3]
            hi = ag.astype(BF16)
            at = lanes(b)
            fi[0:64, at] = hi
            fi[64:128, at] = (ag - hi.astype(F32)).astype(BF16)
            fi[128:192, at] = hi

    TALL = 512

    def half_tiles(h, body):
        ls = pl.ds(pl.multiple_of(h * WIDE, WIDE), WIDE)

        def go(n, _):
            body(pl.ds(pl.multiple_of(n * TALL, TALL), TALL), ls)
            return 0
        lax.fori_loop(0, LONG // TALL, go, 0)

    def score_tile(js, ls):
        s = jnp.dot(kT[js, :], qcat[:, ls], preferred_element_type=F32)
        kern[js, ls] = jnp.exp2(s * EXP2_SCALE)

    def weigh(fresh):
        def body(js, ls):
            w = kern[js, ls] * jnp.dot(lj[js, :], fi[:, ls], preferred_element_type=F32)
            r8[:, ls] += jnp.sum(w.reshape(TALL // 8, 8, WIDE), 0)
            part = w[:, 0:128]
            for n in range(1, HALF):
                part = part + w[:, n * 128:(n + 1) * 128]
            if fresh:
                cacc[js, :] = part
            else:
                cacc[js, :] += part
        return body

    wait_recv(qs, Q_IN, HALF - 1)
    send(own_half(qs), own_half(qs), Q_SIB, sibling)
    prep_q(core)
    half_tiles(core, score_tile)
    wait_recv(gs, G_IN, HALF - 1)
    send(own_half(gs), own_half(gs), G_SIB, sibling)
    wait_recv(qs, Q_SIB, HALF)
    prep_q(1 - core)
    half_tiles(1 - core, score_tile)

    wait_recv(vs, V_IN, GROUP - 1)
    for b in range(GROUP):
        rows = slice(b * BLOCK, (b + 1) * BLOCK)
        scales = vs[b, HEAD:MSG, :].astype(F32)
        for t in range(3):
            b_p[t, b:b + 1, :] = scales[t:t + 1]
        bv = vs[b, 0:HEAD, :].astype(F32) * scales[2:3]
        hi = bv.astype(BF16).astype(F32)
        lj[rows, 0:128] = jnp.concatenate([hi, hi], 0).T.astype(BF16)
        lj[rows, 128:256] = jnp.concatenate([bv - hi, zero], 0).T.astype(BF16)
    prep_g(core)
    half_tiles(core, weigh(True))
    wait_recv(gs, G_SIB, HALF)
    prep_g(1 - core)
    half_tiles(1 - core, weigh(False))

    def column_block(b, acc, r):
        ar[r, me_b, b:b + 1, :] = jnp.sum(acc.T, 0, keepdims=True)

    for b in range(GROUP):
        column_block(b, cacc[b * BLOCK:(b + 1) * BLOCK, :], 0)

    def total(r):
        return jnp.sum(ar[r], 0)

    def spread_keys(dst, src):
        for b in range(GROUP):
            dst[b * BLOCK:(b + 1) * BLOCK, :] = jnp.broadcast_to(src[b:b + 1, :], (BLOCK, BLOCK)).T

    def spread_queries():
        for b in range(GROUP):
            w8[:, b * 128:(b + 1) * 128] = jnp.broadcast_to(vec[b:b + 1, :], (8, BLOCK))

    def column_apply(r):
        for b in range(GROUP):
            at = slice(b * BLOCK, (b + 1) * BLOCK)
            acc = kern[at, 0:128] * w8[0:1, 0:128]
            for n in range(1, GROUP):
                acc = acc + kern[at, n * 128:(n + 1) * 128] * w8[0:1, n * 128:(n + 1) * 128]
            column_block(b, acc, r)

    def row_apply(store):
        def go(c, accs):
            js = pl.ds(pl.multiple_of(c * 64, 64), 64)
            u = ub[js, :]
            return tuple(
                accs[n] + jnp.sum((kern[js, n * 128:(n + 1) * 128] * u).reshape(8, 8, 128), 0)
                for n in range(GROUP))
        accs = lax.fori_loop(
            0, LONG // 64, go, tuple(jnp.zeros((8, BLOCK), F32) for _ in range(GROUP)), unroll=2)
        for n in range(GROUP):
            store(n, accs[n])

    def value_tile(n, _):
        js = pl.ds(pl.multiple_of(n * TALL, TALL), TALL)
        b3 = b3b[js, :]
        scale = fif[63:64, :] * jnp.concatenate([b3] * GROUP, 1)
        probs = (kern[js, :] * scale).astype(BF16)
        gvt[js, :] = jnp.dot(probs, gT[...], preferred_element_type=F32)
        return 0

    def put_rows(dst, rows, value):
        for n, piece in zip(rows, value):
            vec[...] = piece
            for b in range(GROUP):
                dst[n:n + 1, b * 128:(b + 1) * 128] = vec[b:b + 1, :]

    def turn_back(block):
        wide = jnp.concatenate([block, jnp.zeros((BLOCK, BLOCK - HEAD), F32)], 1)
        return wide.T[0:HEAD, :]

    to_xy(ar.at[0], AR)
    put_rows(fif, [63], [a_p[2]])
    spread_keys(b3b, b_p.at[2])
    for b in range(GROUP):
        gT[b * BLOCK:(b + 1) * BLOCK, :] = turned(gs[b, 0:HEAD, :]).astype(BF16)
    lax.fori_loop(0, LONG // TALL, value_tile, 0)

    for t in (2, 1, 0):
        r = 2 * (2 - t)
        wait_recv(ar.at[r], AR + r, GROUP - 1)
        dg = -total(r)
        if t < 2:
            dg = b_p[t] * dg
        bdg = b_p[t] * dg
        vec[...] = bdg
        spread_keys(ub, vec)
        if t == 2:
            def store(n, acc):
                a = a_p[2, n:n + 1, :]
                ar[1, me_a, n:n + 1, :] = a * jnp.sum(acc, 0, keepdims=True) + jnp.sum(
                    r8[:, n * 128:(n + 1) * 128], 0, keepdims=True)
        else:
            def store(n, acc, r=r):
                ar[r + 1, me_a, n:n + 1, :] = jnp.sum(acc, 0, keepdims=True)
        row_apply(store)
        to_zc(ar.at[r + 1], AR + r + 1)
        put_rows(ljf, [3 * (2 - t) + n for n in range(3)], split3(bdg))
        if t == 2:
            for b in range(GROUP):
                gvp[b] = turn_back(gvt[b * BLOCK:(b + 1) * BLOCK, :])
            for dx, dy in FAR_XY:
                send(gvp.at[((x + dx) % 4) * 4 + (y + dy) % 4], gvr.at[me_b], GV, dev_xy(dx, dy))
            gvr[me_b] = gvp[me_b]
        elif t == 1:
            for b in range(GROUP):
                qT[b * BLOCK:(b + 1) * BLOCK, :] = turned(qs[b]).astype(BF16)
            for n, s in ((0, 2), (3, 1), (6, 0)):
                put_rows(fif, [n, n + 1, n + 2], [a_p[s]] * 3)
            for n, s in ((9, 1), (12, 0)):
                put_rows(ljf, [n, n + 1, n + 2], [b_p[s]] * 3)
            ljf[15:18, :] = jnp.ones((3, LONG), F32)
        else:
            for b in range(GROUP):
                rows = slice(b * BLOCK, (b + 1) * BLOCK)
                lj[rows, LOW:LOW + HEAD] = turned(ljf[:, rows]).astype(BF16)
            wait_recv(gvr, GV, GROUP - 1)
            out_ref[2] = jnp.sum(gvr[...], 0)
        wait_recv(ar.at[r + 1], AR + r + 1, GROUP - 1)
        df = -total(r + 1)
        if t < 2:
            df = a_p[t] * df
        adf = a_p[t] * df
        if t > 0:
            vec[...] = adf
            spread_queries()
            column_apply(r + 2)
            to_xy(ar.at[r + 2], AR + r + 2)
        put_rows(fif, [9 + 3 * (2 - t) + n for n in range(3)], split3(adf))

    fi[LOW:LOW + HEAD, :] = fif[...].astype(BF16)

    def last_tile(h, jt, fresh):
        ls = pl.ds(pl.multiple_of(h * WIDE, WIDE), WIDE)
        js = pl.ds(pl.multiple_of(jt * WIDE, WIDE), WIDE)
        bracket = jnp.dot(lj[js, :], fi[:, ls], preferred_element_type=F32)
        ds = (kern[js, ls] * bracket).astype(BF16)
        part = jnp.dot(kcat[:, js], ds, preferred_element_type=F32)
        turn = jnp.dot(ds, qT[ls, :], preferred_element_type=F32)

        @pl.when(jt == 0)
        def _():
            for n in range(HALF):
                gqp[h * HALF + n] = part[:, n * 128:(n + 1) * 128]

        @pl.when(jt > 0)
        def _():
            for n in range(HALF):
                gqp[h * HALF + n] += part[:, n * 128:(n + 1) * 128]
        if fresh:
            gkt[js, :] = turn
            return
        gkt[js, :] += turn
        for n in range(HALF):
            gkp[jt * HALF + n] = turn_back(gkt[lanes(jt * HALF + n), :])

    def send_keys(jt):
        for n in range(HALF):
            p = jt * HALF + n

            @pl.when(p != me_b)
            def _():
                send(gkp.at[p], gkr.at[me_b], GK, ((p // 4) * 2 + core, (p % 4) * 8 + z))

    def last_first(jt, _):
        last_tile(1 - core, jt, True)
        return 0

    lax.fori_loop(0, 2, last_first, 0)
    send(gqp.at[pl.ds(pl.multiple_of((1 - core) * HALF, HALF), HALF)], gqs, GQ_SIB, sibling)

    def last_second(jt, _):
        last_tile(core, jt, False)

        @pl.when(jt == 0)
        def _():
            send_keys(0)
        return 0

    lax.fori_loop(0, 2, last_second, 0)
    wait_recv(gqs, GQ_SIB, HALF)
    for n in range(HALF):
        gqp[core * HALF + n] += gqs[n]
    for dz in FAR_Z:
        to = (z + dz) % 8
        send(gqp.at[core * HALF + to], gqr.at[z], GQ, dev_z(dz, 0))
    send_keys(1)
    gqr[z] = gqp[me_a]
    gkr[me_b] = gkp[me_b]
    wait_recv(gqr, GQ, HALF - 1)
    out_ref[0] = jnp.sum(gqr[...], 0) * SCALE
    wait_recv(gkr, GK, GROUP - 1)
    out_ref[1] = jnp.sum(gkr[...], 0) * SCALE
    wait_send(ks, K_IN, GROUP - 1)
    wait_send(vs, V_IN, GROUP - 1)
    wait_send(qs, Q_IN, HALF - 1)
    wait_send(gs, G_IN, HALF - 1)
    wait_send(qs, Q_SIB, HALF)
    wait_send(gs, G_SIB, HALF)
    for r in range(6):
        wait_send(ar.at[r], AR + r, GROUP - 1)
    wait_send(gvp, GV, GROUP - 1)
    wait_send(gqs, GQ_SIB, HALF)
    wait_send(gqr, GQ, HALF - 1)
    wait_send(gkp, GK, GROUP - 1)


def body(queries, keys, values, out_grads, row_scales, column_scales):
    vmem = pl.BlockSpec(memory_space=pltpu.VMEM)
    parts = [pltpu.VMEM((GROUP, HEAD, BLOCK), F32)] * 3
    half = pltpu.VMEM((HALF, HEAD, BLOCK), F32)
    out = pl.pallas_call(
        kernel,
        out_shape=jax.ShapeDtypeStruct((3, HEAD, BLOCK), F32),
        in_specs=[vmem] * 6,
        out_specs=vmem,
        scratch_shapes=[
            pltpu.VMEM((GROUP, HEAD, BLOCK), BF16),
            pltpu.VMEM((GROUP, MSG, BLOCK), BF16),
            pltpu.VMEM((GROUP, HEAD, BLOCK), BF16),
            pltpu.VMEM((GROUP, MSG, BLOCK), BF16),
            pltpu.VMEM((LONG, LONG), F32),
            pltpu.VMEM((LONG, HEAD), BF16),
            pltpu.VMEM((LONG, HEAD), BF16),
            pltpu.VMEM((LONG, HEAD), BF16),
            pltpu.VMEM((LONG, 4 * HEAD), BF16),
            pltpu.VMEM((4 * HEAD, LONG), BF16),
            pltpu.VMEM((HEAD, LONG), F32),
            pltpu.VMEM((HEAD, LONG), F32),
            pltpu.VMEM((HEAD, LONG), BF16),
            pltpu.VMEM((HEAD, LONG), BF16),
            pltpu.VMEM((3, GROUP, BLOCK), F32),
            pltpu.VMEM((3, GROUP, BLOCK), F32),
            pltpu.VMEM((GROUP, BLOCK), F32),
            pltpu.VMEM((LONG, BLOCK), F32),
            pltpu.VMEM((LONG, BLOCK), F32),
            pltpu.VMEM((8, LONG), F32),
            pltpu.VMEM((8, LONG), F32),
            pltpu.VMEM((LONG, BLOCK), F32),
            pltpu.VMEM((6, GROUP, GROUP, BLOCK), F32),
            pltpu.VMEM((LONG, HEAD), F32),
            pltpu.VMEM((LONG, HEAD), F32),
            *parts, half, half, *parts[:2],
            pltpu.SemaphoreType.DMA((N_SEM,)),
            pltpu.SemaphoreType.DMA((N_SEM,)),
        ],
        compiler_params=pltpu.CompilerParams(
            collective_id=0, has_side_effects=True, vmem_limit_bytes=58 * 2**20),
    )(queries, keys, values, out_grads, row_scales, column_scales)
    return out[0], out[1], out[2]


def solution(mesh):
    in_specs = (
        P(None, ("pb", "ka")),
        P(None, ("ka", "pb")),
        P(None, ("ka", "pb")),
        P(None, ("pb", "ka")),
        P(None, ("pb", "ka")),
        P(None, ("ka", "pb")),
    )
    out_specs = (P(None, ("pb", "ka")), P(None, ("ka", "pb")), P(None, ("ka", "pb")))
    return jax.shard_map(body, mesh=mesh, in_specs=in_specs, out_specs=out_specs, check_vma=False)
```

time: 1010 us -> 82.9 us (0.08); the launches traced: 998 us -> 82.7 us
  blocking collectives: 604 us -> 0 us
  waiting for transfers between devices: 257 us -> 0 us
  matrix products: 101 us -> 0 us
  Pallas kernels: 0 us -> 80.6 us
  between operations: 14.1 us -> 0.64 us
  other arithmetic: 12.8 us -> 0 us
    psum x6 -> x0, blocking collectives: 426 us -> none  [the longest x2 220 us: body(): row_sum = lax.psum(jnp.dot(tile(), b[t - 1] * dg[t], precision=HIGH), 'ka')]
    reduce_scatter x3 -> x0, waiting for transfers between devices: 257 us -> none  [the longest x1 214 us: body(): lax.psum_scatter(query_part, 'ka', scatter_dimension=1, tiled=True)]
    all_gather x6 -> x0, blocking collectives: 178 us -> none  [the longest x1 36.8 us: body(): lax.all_gather(queries, 'ka', axis=1, tiled=True)]
    dot_general x10 -> x0, matrix products: 101 us -> none  [the longest x2 35 us: body(): row_sum = lax.psum(jnp.dot(tile(), b[t - 1] * dg[t], precision=HIGH), 'ka')]
    pallas_call x0 -> x1, Pallas kernels: none -> 80.6 us  [body(): pl.pallas_call(kernel, out_shape=jax.ShapeDtypeStruct((3, HEAD, BLOCK), F...]
    convert_element_type x2 -> x0, other arithmetic: 12.7 us -> none  [the longest x1 12.7 us: body(): dscores = (tile() * bracket).astype(jnp.bfloat16)]
  transfers between devices with their start and end apart: 3 -> 0, of which waited for: 2 -> 0; matrix products, arithmetic and copies ran while one was open for 11% -> 0% of each run, Pallas kernels for 0% -> 0%
where the time goes in v2:
time: 82.9 us; the launch traced here: 82.7 us
  Pallas kernels  80.6 us (97%)
  local copies, waits for them, and re-layouts  1.43 us (2%)
    pallas_call x1, Pallas kernels, body(): pl.pallas_call(kernel, out_shape=jax.ShapeDtypeStruct((3, HEAD, BLOCK), F...  80.6 us

profile of v2, /device:TPU:1, one launch (start us, length us, event | category | flops | bytes accessed | tf_op | source)
XLA Modules:
  0.0 82.7 jit_solution(17827748498625983789)
XLA Ops:
  0.6 80.6 %shard_map.85 = f32[3,64,128]{2,1,0:T(8,128)} custom-call(bf16[64,128]{1,0:T(8,128)(2,1)} %q_ref.1, bf16[64,128]{1,0:T(8,128)(2,1)} %k_ref.1, bf16[64,128]{1,0:T(8,128)(2,1)} %v_ref.1, bf16[64,128]{1,0:T(8,128)(2,1)} %g_ref.1, bf16[3,128]{1,0:T(4,128)(2,1)} %rs_ref.1, bf16[3,128]{1,0:T(4,128)(2,1)} %cs_ref.1), custom_call_target="tpu_custom_call" | custom-call | tf_op jit(solution)/shard_map/pallas_call | solution.py:391
  81.3 1.4 %slice_bitcast_fusion = (f32[64,128]{1,0:T(8,128)}, f32[64,128]{1,0:T(8,128)}, f32[64,128]{1,0:T(8,128)}) fusion(f32[3,64,128]{2,1,0:T(8,128)} %shard_map.85), kind=kLoop, calls=%fused_computation | loop fusion | bytes 196608 | tf_op jit(solution)/shard_map/squeeze | solution.py:429
